TPU v7x, 512 devices: a whole 4x4x16 slice. The times are simulated.
512 devices in a mesh: dp: 64 (over x, z_lo, y), tensor: 8 (over z_hi, core).
Axes of the slice: x: 4, y: 4, z: 16 (z_hi: 4, z_lo: 4; z = z_hi * 4 + z_lo), core: 2. Of those that a mesh axis runs over, the one named last changes fastest.
Arguments:
- grad_a: bfloat16 [64, 8, 1024, 3, 64], P('dp', 'tensor'), may hold values from -70 to 70
- grad_b: bfloat16 [64, 64, 8, 1280], P('dp', None, 'tensor'), may hold values from -70 to 70
- params_a: float32 [8, 1024, 3, 64], P('tensor', 'dp'), may hold values from -0.0625 to 0.0625
- params_b: float32 [64, 8, 1280], P('dp', 'tensor'), may hold values from -0.75 to 0.75
- moment_a: float32 [8, 1024, 3, 64], P('tensor', 'dp'), may hold values from -0.00012207031 to 0.00012207031
- moment_b: float32 [64, 8, 1280], P('dp', 'tensor'), may hold values from -0.00012207031 to 0.00012207031
- second_a: float32 [8, 1024, 3, 64], P('tensor', 'dp'), may hold values from 1e-08 to 1e-07
- second_b: float32 [64, 8, 1280], P('dp', 'tensor'), may hold values from 1e-08 to 1e-07
- hidden_in: bfloat16 [4, 512, 8192], P(None, 'dp'), may hold values from -6 to 6
- base_q: bfloat16 [4, 512, 8, 1024], P(None, 'dp', 'tensor'), may hold values from -32 to 32
- base_kv: bfloat16 [4, 512, 8, 256], P(None, 'dp', 'tensor'), may hold values from -6 to 6
- cache_keys: bfloat16 [512, 8, 512, 128], P('dp', 'tensor'), may hold values from -17 to 17
- cache_values: bfloat16 [512, 8, 512, 128], P('dp', 'tensor'), may hold values from -6 to 6
- lengths: int32 [512], P('dp'), may hold values from 2 to 512, as said below
Outputs:
- attention: bfloat16 [4, 512, 8, 1024], P(None, 'dp', 'tensor')
- new_a: float32 [8, 1024, 3, 64], P('tensor', 'dp')
- new_b: float32 [64, 8, 1280], P('dp', 'tensor')
Inputs may be any that keep to these rules, and one draw needn't show every extreme that they name: `lengths`: the first of each block of 8 rows holds exactly 512.
All inputs are finite; a program needn't handle non-finite values.
Results may differ from a plain program's by a relative error of at most 0.017.
The roundings to bfloat16 on the way count: a program that leaves them out, or rounds other values in their place, can miss the bound.
Values may be sent and summed in bfloat16 or wider, within the bound.
No kernel may reach another device: no remote copies, remote signals or barrier semaphores. Data moves between devices by JAX's collectives and lax.ppermute only.
A program may use at most 64 MiB of HBM per device.

v0:
```python
import jax
import jax.numpy as jnp
from jax import lax
from jax.sharding import PartitionSpec as P

D = 8192
R = 64
QUERY_PER_KV = 8
HEAD_SIZE = 128


first_fix = 0.9999734386011124
second_fix = 0.09520785288629038


def adam_update(param, moment, second, grad, clip):
    grad = grad * clip
    moment = 0.9 * moment + 0.1 * grad
    second = 0.999 * second + 0.001 * grad * grad
    first_hat = moment / first_fix
    second_hat = second / second_fix
    return param - 0.1 * first_hat / (jnp.sqrt(second_hat) + 1e-08)


def attend_step(query, key, value, cache_keys, cache_values, lengths, step):
    rows = query.shape[1]
    heads = query.shape[2]
    slots = cache_keys.shape[2]
    q_now = query[step].reshape(rows, heads, QUERY_PER_KV, HEAD_SIZE)
    inv = HEAD_SIZE ** (-0.5)
    cached = (
        jnp.einsum("bhgd,bhpd->bhgp", q_now, cache_keys, preferred_element_type=jnp.float32) * inv
    )
    live = jnp.arange(slots)[None, :] < lengths[:, None]
    cached = jnp.where(live[:, None, None, :], cached, -jnp.inf)
    fresh = (
        jnp.einsum("bhgd,sbhd->bhgs", q_now, key[: step + 1], preferred_element_type=jnp.float32)
        * inv
    )
    top = jnp.maximum(jnp.max(cached, axis=-1), jnp.max(fresh, axis=-1))
    e_cached = jnp.exp(cached - top[..., None])
    e_fresh = jnp.exp(fresh - top[..., None])
    total = jnp.sum(e_cached, axis=-1) + jnp.sum(e_fresh, axis=-1)
    out = jnp.einsum(
        "bhgp,bhpd->bhgd",
        e_cached.astype(jnp.bfloat16),
        cache_values,
        preferred_element_type=jnp.float32,
    )
    out = out + jnp.einsum(
        "bhgs,sbhd->bhgd",
        e_fresh.astype(jnp.bfloat16),
        value[: step + 1],
        preferred_element_type=jnp.float32,
    )
    out = out / total[..., None]
    return out.astype(jnp.bfloat16).reshape(rows, heads, QUERY_PER_KV * HEAD_SIZE)


def shards(
    grad_a,
    grad_b,
    params_a,
    params_b,
    moment_a,
    moment_b,
    second_a,
    second_b,
    hidden_in,
    base_q,
    base_kv,
    cache_keys,
    cache_values,
    lengths,
):
    replicas = lax.axis_size("dp")
    summed_a, summed_b = (
        lax.psum_scatter(grad_a.astype(jnp.float32), "dp", scatter_dimension=2, tiled=True),
        lax.psum_scatter(grad_b.astype(jnp.float32), "dp", scatter_dimension=1, tiled=True),
    )
    mean_a = summed_a[0] / replicas
    mean_b = summed_b[0] / replicas
    squares = lax.psum(jnp.sum(mean_a * mean_a) + jnp.sum(mean_b * mean_b), ("dp", "tensor"))
    clip = jnp.minimum(1.0, 1.0 / (jnp.sqrt(squares) + 1e-06))
    new_a = adam_update(params_a, moment_a, second_a, mean_a, clip)
    new_b = adam_update(params_b, moment_b, second_b, mean_b, clip)
    adapter_a, adapter_b = (
        lax.all_gather(new_a.astype(jnp.bfloat16), "dp", axis=1, tiled=True),
        lax.all_gather(new_b.astype(jnp.bfloat16), "dp", axis=0, tiled=True),
    )
    steps, rows = (hidden_in.shape[0], hidden_in.shape[1])
    flat = hidden_in.reshape(steps * rows, D)
    width = adapter_a.shape[1]
    piece = lax.all_gather(adapter_a, "tensor", axis=0, tiled=True)
    count = piece.shape[0] * width
    clip_factor = jnp.dot(flat, piece.reshape(count, 3 * R), preferred_element_type=jnp.float32)
    clip_factor = clip_factor.astype(jnp.bfloat16).reshape(steps, rows, 3, R)
    query_delta = jnp.einsum(
        "alo,oei->alei",
        clip_factor[:, :, 0],
        adapter_b[:, :, : QUERY_PER_KV * HEAD_SIZE],
        preferred_element_type=jnp.float32,
    )
    key_delta = jnp.einsum(
        "alo,oei->alei",
        clip_factor[:, :, 1],
        adapter_b[:, :, QUERY_PER_KV * HEAD_SIZE : (QUERY_PER_KV + 1) * HEAD_SIZE],
        preferred_element_type=jnp.float32,
    )
    value_delta = jnp.einsum(
        "alo,oei->alei",
        clip_factor[:, :, 2],
        adapter_b[:, :, (QUERY_PER_KV + 1) * HEAD_SIZE :],
        preferred_element_type=jnp.float32,
    )
    query = (base_q.astype(jnp.float32) + 2.0 * query_delta).astype(jnp.bfloat16)
    key = (base_kv[..., :HEAD_SIZE].astype(jnp.float32) + 2.0 * key_delta).astype(jnp.bfloat16)
    value = (base_kv[..., HEAD_SIZE:].astype(jnp.float32) + 2.0 * value_delta).astype(jnp.bfloat16)
    outputs = [
        attend_step(query, key, value, cache_keys, cache_values, lengths, step)
        for step in range(steps)
    ]
    return (jnp.stack(outputs), new_a, new_b)


def solution(mesh):
    in_specs = (
        P("dp", "tensor", None, None, None),
        P("dp", None, "tensor", None),
        P("tensor", "dp", None, None),
        P("dp", "tensor", None),
        P("tensor", "dp", None, None),
        P("dp", "tensor", None),
        P("tensor", "dp", None, None),
        P("dp", "tensor", None),
        P(None, "dp", None),
        P(None, "dp", "tensor", None),
        P(None, "dp", "tensor", None),
        P("dp", "tensor", None, None),
        P("dp", "tensor", None, None),
        P("dp"),
    )
    out_specs = (
        P(None, "dp", "tensor", None),
        P("tensor", "dp", None, None),
        P("dp", "tensor", None),
    )
    return jax.shard_map(shards, mesh=mesh, in_specs=in_specs, out_specs=out_specs, check_vma=False)
```

profile of v0, /device:TPU:8, one launch (start us, length us, event | category | flops | bytes accessed | tf_op | source)
XLA Modules:
  0.0 1249.2 jit_solution(1674090310146882115)
XLA Ops:
  7.2 0.0 copy-start
  7.3 0.0 all-reduce.5.cloned.1.call-start
  7.3 4.5 copy.129
  11.8 0.0 all-reduce.5.cloned.1.call-update
  11.8 0.0 all-gather.2.cloned.1.call-start
  11.9 1.3 dynamic-slice
  13.8 364.9 %all-reduce.6 = f32[1,64,1,1280]{3,1,2,0:T(8,128)S(1)} all-reduce(bf16[1,64,1,1280]{3,1,2,0:T(8,128)(2,1)S(1)} %copy-done.4), channel_id=3, replica_groups=mesh['dp'=64,'tensor'=8] {'dp'}, use_global_device_ids=true, to_apply=%region_2.0.clone | all-reduce | flops 81920 | bytes 491520
  378.7 1.3 multiply_reduce_fusion.1
  380.0 361.4 %all-reduce.5.cloned.1.call-done = f32[1,1,1024,3,64]{4,1,3,0,2:T(1,128)} async-done(((f32[1,1,1024,3,64]{4,1,3,0,2:T(1,128)}), f32[1,1,1024,3,64]{4,1,3,0,2:T(1,128)}) %all-reduce.5.cloned.1.call-update) | async-done | bytes 786448
  741.4 1.4 multiply_reduce_fusion
  744.1 103.4 %psum.7 = f32[]{:T(128)} all-reduce(f32[]{:T(128)S(6)} %add.95), channel_id=1, replica_groups=mesh['dp'=64,'tensor'=8] {'dp','tensor'}, use_global_device_ids=true, to_apply=%region_4.0 | all-reduce | flops 1 | bytes 8 | tf_op jit(solution)/shard_map/psum | solution.py:83
  848.2 0.9 fusion.89
  849.2 183.9 %all_gather.9 = bf16[1,1024,3,64]{3,1,2,0:T(8,128)(2,1)S(1)} all-gather(bf16[1,16,3,64]{3,1,2,0:T(8,128)(2,1)S(1)} %copy.132), channel_id=1, replica_groups=mesh['dp'=64,'tensor'=8] {'dp'}, dimensions={1}, use_global_device_ids=true | all-gather | bytes 399360 | tf_op jit(solution)/shard_map/all_gather | solution.py:88
  1033.1 1.0 copy.133
  1034.1 0.0 all-gather.2.cloned.1.call-update
  1034.1 0.1 iota_compare_fusion
  1034.2 1.3 fusion.90
  1035.5 192.6 %all_gather.11 = bf16[64,1,1280]{2,1,0:T(2,128)(2,1)S(1)} all-gather(bf16[1,1,1280]{2,1,0:T(2,128)(2,1)S(1)} %get-tuple-element.20), channel_id=1, replica_groups=mesh['dp'=64,'tensor'=8] {'dp'}, dimensions={0}, use_global_device_ids=true | all-gather | bytes 166400 | tf_op jit(solution)/shard_map/all_gather | solution.py:89
  1228.1 0.7 copy.156
  1228.7 0.1 fusion.92
  1228.8 0.0 all-gather.2.cloned.1.call-done
  1228.8 3.6 copy.134
  1232.5 2.2 copy.167
  1234.7 1.1 fusion.15
  1235.8 0.1 reshape.414
  1235.9 0.1 fusion.21
  1236.1 0.1 fusion.20
  1236.2 0.2 fusion.6
  1236.4 0.1 fusion.99
  1236.6 0.5 fusion.98
  1237.0 0.2 fusion.36
  1237.2 0.3 fusion.26
  1237.5 0.5 fusion.96
  1238.0 0.1 fusion.97
  1238.2 0.2 fusion.38
  1238.3 0.3 fusion.24
  1238.6 0.5 fusion.94
  1239.1 0.1 fusion.95
  1239.3 0.2 fusion.40
  1239.4 0.3 fusion.22
  1239.7 0.5 fusion.100
  1240.2 0.1 fusion.60
  1240.4 0.2 fusion.34
  1240.6 0.3 fusion.11
  1240.9 0.2 fusion.12
  1241.2 0.2 fusion.13
  1241.5 0.2 fusion.14
  1241.7 0.6 pad_maximum_fusion
  (53 shorter events, 0.3 us)
Async XLA Ops:
  7.2 1229.4 %copy-start = (bf16[8,1,512,128]{3,2,1,0:T(8,128)(2,1)S(1)}, bf16[8,1,512,128]{3,2,1,0:T(8,128)(2,1)}, u32[]{:S(2)}) copy-start(bf16[8,1,512,128]{3,2,1,0:T(8,128)(2,1)} %param.25) | copy-start | bytes 3145732
  7.2 6.6 copy-start.4
  7.2 841.0 %copy-start.8 = (f32[1,16,3,64]{3,1,2,0:T(8,128)S(1)}, f32[1,16,3,64]{3,1,2,0:T(8,128)}, u32[]{:S(2)}) copy-start(f32[1,16,3,64]{3,1,2,0:T(8,128)} %param.16) | copy-start | bytes 36868
  7.2 841.0 %copy-start.7 = (f32[1,16,3,64]{3,1,2,0:T(8,128)S(1)}, f32[1,16,3,64]{3,1,2,0:T(8,128)}, u32[]{:S(2)}) copy-start(f32[1,16,3,64]{3,1,2,0:T(8,128)} %param.18) | copy-start | bytes 36868
  7.2 841.0 %copy-start.6 = (f32[1,16,3,64]{3,1,2,0:T(8,128)S(1)}, f32[1,16,3,64]{3,1,2,0:T(8,128)}, u32[]{:S(2)}) copy-start(f32[1,16,3,64]{3,1,2,0:T(8,128)} %param.20) | copy-start | bytes 36868
  7.2 1026.9 %copy-start.13 = (s32[8]{0:T(128)S(1)}, s32[8]{0:T(128)}, u32[]{:S(2)}) copy-start(s32[8]{0:T(128)} %param.27) | copy-start | bytes 100
  7.2 1027.0 %copy-start.10 = (f32[1,1,1280]{2,1,0:T(1,128)S(1)}, f32[1,1,1280]{2,1,0:T(1,128)}, u32[]{:S(2)}) copy-start(f32[1,1,1280]{2,1,0:T(1,128)} %param.17) | copy-start | bytes 15364
  7.2 1027.0 %copy-start.12 = (f32[1,1,1280]{2,1,0:T(1,128)S(1)}, f32[1,1,1280]{2,1,0:T(1,128)}, u32[]{:S(2)}) copy-start(f32[1,1,1280]{2,1,0:T(1,128)} %param.19) | copy-start | bytes 15364
  7.3 1027.0 %copy-start.11 = (f32[1,1,1280]{2,1,0:T(1,128)S(1)}, f32[1,1,1280]{2,1,0:T(1,128)}, u32[]{:S(2)}) copy-start(f32[1,1,1280]{2,1,0:T(1,128)} %param.21) | copy-start | bytes 15364
  7.3 734.1 %all-reduce.5.cloned.1.call-start = ((), (), s32[]{:S(2)}) async-start(), calls=%async_computation.1 | async-start | bytes 3145728
  11.8 1217.0 %all-gather.2.cloned.1.call-start = ((), (), s32[]{:S(2)}) async-start(), calls=%async_computation | async-start | bytes 3538944 | tf_op jit(solution)/shard_map/all_gather | solution.py:94
  1228.1 4.4 copy-start.2
  1232.5 2.2 copy-start.3
  1234.7 1.3 copy-start.9
  1234.7 1.5 slice-start
  1234.7 1.5 copy-start.5
  1234.7 2.5 copy-start.1
Sparse Core Ops, SparseCore 0:
  11.9 729.3 all-reduce.4
  1034.2 71.0 all-gather.1
where the time goes:
time: 1250 us
  blocking collectives  845 us (68%)
  waiting for transfers between devices  361 us (29%)
  between operations  17.1 us (1%)
  local copies, waits for them, and re-layouts  13.6 us (1%)
    unnamed x1, blocking collectives  365 us
    unnamed x3, waiting for transfers between devices  361 us
    all_gather x1, blocking collectives, shards(): lax.all_gather(new_b.astype(jnp.bfloat16), 'dp', axis=0, tiled=True)  193 us
    all_gather x1, blocking collectives, shards(): lax.all_gather(new_a.astype(jnp.bfloat16), 'dp', axis=1, tiled=True)  184 us
    psum x1, blocking collectives, shards(): lax.psum(jnp.sum(mean_a * mean_a) + jnp.sum(mean_b * mean_b), ('dp', 'ten...  103 us
  transfers between devices with their start and end apart: 2, of which 1 were waited for; matrix products, arithmetic and copies ran while one was open for 0% of the time, Pallas kernels for 0%

commit v1 on v0

--- a/solution.py
+++ b/solution.py
@@ -74,27 +74,38 @@
     lengths,
 ):
     replicas = lax.axis_size("dp")
-    summed_a, summed_b = (
-        lax.psum_scatter(grad_a.astype(jnp.float32), "dp", scatter_dimension=2, tiled=True),
-        lax.psum_scatter(grad_b.astype(jnp.float32), "dp", scatter_dimension=1, tiled=True),
+    devices = replicas * lax.axis_size("tensor")
+    local_a = params_a.size
+    rows_a = grad_a.reshape(replicas, local_a)
+    rows_b = grad_b.reshape(replicas, params_b.size)
+    sent = jnp.concatenate([rows_a, rows_b], axis=1)
+    arrived = lax.all_to_all(sent, "dp", 0, 0, tiled=True)
+    mean = jnp.sum(arrived.astype(jnp.float32), axis=0) / replicas
+    squares = jnp.broadcast_to(jnp.sum(mean * mean), (devices, 1, 128))
+    squares = lax.all_to_all(squares, ("dp", "tensor"), 0, 0, tiled=True)
+    squares = jnp.sum(squares[:, 0, 0])
+    clip = jnp.minimum(1.0, 1.0 / (jnp.sqrt(squares) + 1e-06))
+    new_a = adam_update(params_a, moment_a, second_a, mean[:local_a].reshape(params_a.shape), clip)
+    new_b = adam_update(params_b, moment_b, second_b, mean[local_a:].reshape(params_b.shape), clip)
+    shard = jnp.concatenate([new_a.reshape(-1), new_b.reshape(-1)]).astype(jnp.bfloat16)
+    adapters = lax.all_to_all(
+        jnp.broadcast_to(shard, (replicas, shard.size)), "dp", 0, 0, tiled=True
     )
-    mean_a = summed_a[0] / replicas
-    mean_b = summed_b[0] / replicas
-    squares = lax.psum(jnp.sum(mean_a * mean_a) + jnp.sum(mean_b * mean_b), ("dp", "tensor"))
-    clip = jnp.minimum(1.0, 1.0 / (jnp.sqrt(squares) + 1e-06))
-    new_a = adam_update(params_a, moment_a, second_a, mean_a, clip)
-    new_b = adam_update(params_b, moment_b, second_b, mean_b, clip)
-    adapter_a, adapter_b = (
-        lax.all_gather(new_a.astype(jnp.bfloat16), "dp", axis=1, tiled=True),
-        lax.all_gather(new_b.astype(jnp.bfloat16), "dp", axis=0, tiled=True),
+    adapter_a = adapters[:, :local_a].reshape(-1, 3 * R)
+    adapter_b = adapters[:, local_a:].reshape(replicas, 1, -1)
+    steps, rows = (hidden_in.shape[0], hidden_in.shape[1])
+    width = adapter_a.shape[0]
+    mine = lax.dynamic_slice_in_dim(hidden_in, lax.axis_index("tensor") * width, width, axis=2)
+    partial = jnp.dot(
+        mine.reshape(steps * rows, width), adapter_a, preferred_element_type=jnp.float32
     )
-    steps, rows = (hidden_in.shape[0], hidden_in.shape[1])
-    flat = hidden_in.reshape(steps * rows, D)
-    width = adapter_a.shape[1]
-    piece = lax.all_gather(adapter_a, "tensor", axis=0, tiled=True)
-    count = piece.shape[0] * width
-    clip_factor = jnp.dot(flat, piece.reshape(count, 3 * R), preferred_element_type=jnp.float32)
-    clip_factor = clip_factor.astype(jnp.bfloat16).reshape(steps, rows, 3, R)
+    groups = lax.axis_size("tensor")
+    partial = lax.all_to_all(
+        jnp.broadcast_to(partial.reshape(-1, 128), (groups, partial.size // 128, 128)),
+        "tensor", 0, 0, tiled=True,
+    )
+    shrink = jnp.sum(partial, axis=0).astype(jnp.bfloat16)
+    clip_factor = shrink.reshape(steps, rows, 3, R)
     query_delta = jnp.einsum(
         "alo,oei->alei",
         clip_factor[:, :, 0],

time: 1250 us -> 145 us (0.12)
  the two profiles are of different devices: /device:TPU:8 before, /device:TPU:33 now
where the time goes in v1:
time: 145 us; the launch traced here: 144 us
  blocking collectives  70.6 us (49%)
  waiting for transfers between devices  33.9 us (23%)
  starting transfers between devices  12.5 us (9%)
  other arithmetic  10.9 us (8%)
  local copies, waits for them, and re-layouts  8.43 us (6%)
  matrix products  5.68 us (4%)
  between operations  1.82 us (1%)
    all_to_all x1, blocking collectives, shards(): squares = lax.all_to_all(squares, ('dp', 'tensor'), 0, 0, tiled=True)  44.4 us
    all_to_all x1, blocking collectives, shards(): arrived = lax.all_to_all(sent, 'dp', 0, 0, tiled=True)  26.2 us
    all_to_all x1, waiting for transfers between devices, shards(): lax.all_to_all(jnp.broadcast_to(partial.reshape(-1, 128), (groups, partia...  18.7 us
    all_to_all x1, waiting for transfers between devices, shards(): lax.all_to_all(jnp.broadcast_to(shard, (replicas, shard.size)), 'dp', 0,...  15.2 us
    all_to_all x1, starting transfers between devices, shards(): lax.all_to_all(jnp.broadcast_to(partial.reshape(-1, 128), (groups, partia...  6.56 us
    all_to_all x1, starting transfers between devices, shards(): lax.all_to_all(jnp.broadcast_to(shard, (replicas, shard.size)), 'dp', 0,...  5.89 us
    broadcast_in_dim x1, other arithmetic, shards(): jnp.broadcast_to(shard, (replicas, shard.size))  4 us
    unnamed x30, local copies, waits for them, and re-layouts  3.83 us
  transfers between devices with their start and end apart: 2, of which 2 were waited for; matrix products, arithmetic and copies ran while one was open for 0% of the time, Pallas kernels for 0%

profile of v1, /device:TPU:33, one launch (start us, length us, event | category | flops | bytes accessed | tf_op | source)
XLA Modules:
  0.0 143.8 jit_solution(752352949707800650)
XLA Ops:
  0.7 1.7 %copy.159 = bf16[1,1,1024,3,64]{4,3,2,1,0:T(4,128)(2,1)S(1)} copy(bf16[1,1,1024,3,64]{2,4,3,1,0:T(8,128)(2,1)} %param.14) | data formatting | bytes 786432 | tf_op args[0]
  2.4 0.9 reshape.378
  3.3 0.5 broadcast.124
  3.8 1.0 reduce.32
  4.9 0.1 reshape.409
  5.0 26.2 %all_to_all.28 = bf16[64,2,2176]{2,1,0:T(2,128)(2,1)S(1)} all-to-all(bf16[64,2,2176]{2,1,0:T(2,128)(2,1)S(1)} %reshape.409), channel_id=1, replica_groups=mesh['dp'=64,'tensor'=8] {'dp'}, dimensions={0} | all-to-all | bytes 1114112 | tf_op jit(solution)/shard_map/all_to_all | solution.py:82
  31.2 0.5 reshape.410
  31.7 1.2 convert_reduce_fusion
  33.0 0.6 multiply_reduce_fusion
  33.6 0.8 broadcast_in_dim.31
  34.4 44.4 %all_to_all.29 = f32[512,1,128]{2,1,0:T(1,128)S(1)} all-to-all(f32[512,1,128]{2,1,0:T(1,128)S(1)} %broadcast_in_dim.31), channel_id=1, replica_groups=mesh['dp'=64,'tensor'=8] {'dp','tensor'}, dimensions={0} | all-to-all | bytes 524288 | tf_op jit(solution)/shard_map/all_to_all | solution.py:85
  78.8 1.1 slice_reduce_fusion
  80.8 0.6 fusion.89
  81.5 0.6 convert_reduce_fusion.1
  82.2 0.6 broadcast_in_dim.32
  82.8 4.0 %reduce.33 = bf16[64,4352]{1,0:T(8,128)(2,1)S(1)} reduce(bf16[64,1,4352]{2,1,0:T(2,128)(2,1)S(1)} %broadcast_in_dim.32, bf16[]{:T(256)} %broadcast.124), dimensions={1}, to_apply=%broadcast_in_dim.32.reduce_sub_computation | reduce | bytes 1114114 | tf_op jit(solution)/shard_map/broadcast_in_dim | solution.py:92
  86.8 0.9 reshape.411
  87.7 5.9 %all-to-all-start.2 = ((bf16[64,2,2176]{2,1,0:T(2,128)(2,1)}), bf16[64,2,2176]{2,1,0:T(2,128)(2,1)S(1)}, u32[]{:S(2)}, u32[]{:S(2)}) async-start(bf16[64,2,2176]{2,1,0:T(2,128)(2,1)} %reshape.411), calls=%async_computation.2 | async-start | bytes 1114112 | tf_op jit(solution)/shard_map/all_to_all | solution.py:91
  93.6 15.2 %all-to-all-done.2 = bf16[64,2,2176]{2,1,0:T(2,128)(2,1)S(1)} async-done(((bf16[64,2,2176]{2,1,0:T(2,128)(2,1)}), bf16[64,2,2176]{2,1,0:T(2,128)(2,1)S(1)}, u32[]{:S(2)}, u32[]{:S(2)}) %all-to-all-start.2) | async-done | bytes 557088 | tf_op jit(solution)/shard_map/all_to_all | solution.py:91
  108.8 0.5 reshape.412
  109.3 0.6 reshape.382
  110.0 1.1 fusion.44
  111.1 0.7 broadcast_in_dim.33
  111.8 6.6 %all-to-all-start.3 = ((f32[8,48,128]{2,1,0:T(8,128)}), f32[8,48,128]{2,1,0:T(8,128)S(1)}, u32[]{:S(2)}, u32[]{:S(2)}) async-start(f32[8,48,128]{2,1,0:T(8,128)} %broadcast_in_dim.33), calls=%async_computation.3 | async-start | bytes 393216 | tf_op jit(solution)/shard_map/all_to_all | solution.py:103
  118.5 18.7 %all-to-all-done.3 = f32[8,48,128]{2,1,0:T(8,128)S(1)} async-done(((f32[8,48,128]{2,1,0:T(8,128)}), f32[8,48,128]{2,1,0:T(8,128)S(1)}, u32[]{:S(2)}, u32[]{:S(2)}) %all-to-all-start.3) | async-done | bytes 196640 | tf_op jit(solution)/shard_map/all_to_all | solution.py:103
  137.4 0.1 fusion.20
  137.5 0.1 fusion.19
  137.7 0.2 fusion.6
  137.9 0.1 fusion.97
  138.0 0.5 fusion.96
  138.5 0.2 fusion.34
  138.7 0.3 fusion.25
  139.0 0.5 fusion.94
  139.4 0.1 fusion.95
  139.6 0.2 fusion.36
  139.8 0.3 fusion.23
  140.1 0.5 fusion.92
  140.5 0.1 fusion.93
  140.7 0.2 fusion.38
  140.9 0.3 fusion.21
  141.2 0.5 fusion.98
  141.7 0.1 fusion.63
  141.8 0.2 fusion.32
  142.0 0.3 fusion.11
  142.4 0.2 fusion.12
  142.6 0.2 fusion.13
  142.9 0.2 fusion.14
  143.1 0.6 pad_maximum_fusion
  (61 shorter events, 1.0 us)
Async XLA Ops:
  0.6 137.4 %copy-start = (bf16[8,1,512,128]{3,2,1,0:T(8,128)(2,1)S(1)}, bf16[8,1,512,128]{3,2,1,0:T(8,128)(2,1)}, u32[]{:S(2)}) copy-start(bf16[8,1,512,128]{3,2,1,0:T(8,128)(2,1)} %param.25) | copy-start | bytes 3145732
  0.6 2.6 %copy-start.2 = (bf16[1,64,1,1280]{3,1,2,0:T(8,128)(2,1)S(1)}, bf16[1,64,1,1280]{3,1,2,0:T(8,128)(2,1)}, u32[]{:S(2)}) copy-start(bf16[1,64,1,1280]{3,1,2,0:T(8,128)(2,1)} %param.15) | copy-start | bytes 491524
  31.7 49.1 %copy-start.4 = (f32[1,16,3,64]{3,1,2,0:T(8,128)S(1)}, f32[1,16,3,64]{3,1,2,0:T(8,128)}, u32[]{:S(2)}) copy-start(f32[1,16,3,64]{3,1,2,0:T(8,128)} %param.16) | copy-start | bytes 36868
  31.7 49.1 %copy-start.5 = (f32[1,16,3,64]{3,1,2,0:T(8,128)S(1)}, f32[1,16,3,64]{3,1,2,0:T(8,128)}, u32[]{:S(2)}) copy-start(f32[1,16,3,64]{3,1,2,0:T(8,128)} %param.20) | copy-start | bytes 36868
  31.7 49.1 %copy-start.6 = (f32[1,16,3,64]{3,1,2,0:T(8,128)S(1)}, f32[1,16,3,64]{3,1,2,0:T(8,128)}, u32[]{:S(2)}) copy-start(f32[1,16,3,64]{3,1,2,0:T(8,128)} %param.18) | copy-start | bytes 36868
  31.7 49.8 %copy-start.8 = (f32[1,1,1280]{2,1,0:T(1,128)S(1)}, f32[1,1,1280]{2,1,0:T(1,128)}, u32[]{:S(2)}) copy-start(f32[1,1,1280]{2,1,0:T(1,128)} %param.17) | copy-start | bytes 15364
  31.7 49.8 %copy-start.9 = (f32[1,1,1280]{2,1,0:T(1,128)S(1)}, f32[1,1,1280]{2,1,0:T(1,128)}, u32[]{:S(2)}) copy-start(f32[1,1,1280]{2,1,0:T(1,128)} %param.21) | copy-start | bytes 15364
  31.7 49.8 %copy-start.10 = (f32[1,1,1280]{2,1,0:T(1,128)S(1)}, f32[1,1,1280]{2,1,0:T(1,128)}, u32[]{:S(2)}) copy-start(f32[1,1,1280]{2,1,0:T(1,128)} %param.19) | copy-start | bytes 15364
  87.7 21.1 %all-to-all-start.2 = ((bf16[64,2,2176]{2,1,0:T(2,128)(2,1)}), bf16[64,2,2176]{2,1,0:T(2,128)(2,1)S(1)}, u32[]{:S(2)}, u32[]{:S(2)}) async-start(bf16[64,2,2176]{2,1,0:T(2,128)(2,1)} %reshape.411), calls=%async_computation.2 | async-start | bytes 1114112 | tf_op jit(solution)/shard_map/all_to_all | solution.py:91
  109.3 9.1 %copy-start.11 = (s32[8]{0:T(128)S(1)}, s32[8]{0:T(128)}, u32[]{:S(2)}) copy-start(s32[8]{0:T(128)} %param.27) | copy-start | bytes 100
  110.0 27.4 %copy-start.7 = (bf16[4,8,1,256]{3,1,2,0:T(8,128)(2,1)S(1)}, bf16[4,8,1,256]{3,1,2,0:T(8,128)(2,1)}, u32[]{:S(2)}) copy-start(bf16[4,8,1,256]{3,1,2,0:T(8,128)(2,1)} %param.24) | copy-start | bytes 49156
  110.0 27.7 %copy-start.3 = (bf16[4,8,1,1024]{3,1,2,0:T(8,128)(2,1)S(1)}, bf16[4,8,1,1024]{3,1,2,0:T(8,128)(2,1)}, u32[]{:S(2)}) copy-start(bf16[4,8,1,1024]{3,1,2,0:T(8,128)(2,1)} %param.23) | copy-start | bytes 196612
  111.8 25.4 %all-to-all-start.3 = ((f32[8,48,128]{2,1,0:T(8,128)}), f32[8,48,128]{2,1,0:T(8,128)S(1)}, u32[]{:S(2)}, u32[]{:S(2)}) async-start(f32[8,48,128]{2,1,0:T(8,128)} %broadcast_in_dim.33), calls=%async_computation.3 | async-start | bytes 393216 | tf_op jit(solution)/shard_map/all_to_all | solution.py:103
  118.5 20.2 %copy-start.1 = (bf16[8,1,512,128]{3,2,1,0:T(8,128)(2,1)S(1)}, bf16[8,1,512,128]{3,2,1,0:T(8,128)(2,1)}, u32[]{:S(2)}) copy-start(bf16[8,1,512,128]{3,2,1,0:T(8,128)(2,1)} %param.26) | copy-start | bytes 3145732

commit v2 on v0

v2 whole, which is shorter than its diff:
```python
import jax
import jax.numpy as jnp
import numpy as np
from jax import lax
from jax.experimental import pallas as pl
from jax.experimental.pallas import tpu as pltpu
from jax.sharding import Mesh
from jax.sharding import PartitionSpec as P

D = 8192
R = 64
QUERY_PER_KV = 8
HEAD_SIZE = 128
STEPS = 4
ROWS = 8
CACHE = 512
TOKENS = STEPS * ROWS
REPLICAS = 64
GROUPS = 8

first_fix = 0.9999734386011124
second_fix = 0.09520785288629038

DP = ("x", "zl", "y")
TENSOR = ("zh", "c")
PLANE = ("x", "y")
NX, NZ, NY = 4, 4, 4
NP = NX * NY

A1, A2, B0 = 0, 64, 96
BLOCK = 136
PADDED = 144
BROWS = PADDED - B0
CHUNKS = 10
OWN1, OWN2, OWN3 = 136, 184, 208
ROW = 240


def shard_id(x, y, z):
    return (x * NZ + z) * NY + y


def tables():
    spread = np.zeros((NP * BROWS, CHUNKS * R), np.float32)
    rank = np.zeros((R, NP * BROWS), np.float32)
    chunk = np.full((1, NP * BROWS), -1, np.int32)
    for x in range(NX):
        for y in range(NY):
            for z in range(NZ):
                d = shard_id(x, y, z)
                for c in range(CHUNKS):
                    row = (x * NY + y) * BROWS + z * CHUNKS + c
                    spread[row, c * R + d] = 1.0
                    rank[d, row] = 1.0
                    chunk[0, row] = c
    order = np.zeros((QUERY_PER_KV * TOKENS,) * 2, np.float32)
    for b in range(ROWS):
        for g in range(QUERY_PER_KV):
            for t in range(STEPS):
                row = (b * QUERY_PER_KV + g) * STEPS + t
                order[row, (g * STEPS + t) * ROWS + b] = 1.0
    return spread, rank, chunk, order


def call(kernel, out_shape, *args, smem=()):
    vmem = pl.BlockSpec(memory_space=pltpu.VMEM)
    scalar = pl.BlockSpec(memory_space=pltpu.SMEM)
    many = isinstance(out_shape, (tuple, list))
    return pl.pallas_call(
        kernel,
        out_shape=out_shape,
        in_specs=[scalar if i in smem else vmem for i in range(len(args))],
        out_specs=[vmem] * len(out_shape) if many else vmem,
        compiler_params=pltpu.CompilerParams(vmem_limit_bytes=48 * 1024 * 1024),
    )(*args)


def dot(a, b):
    return jnp.dot(a, b, preferred_element_type=jnp.float32)


def dot_nt(a, b):
    return lax.dot_general(a, b, (((1,), (1,)), ((), ())), preferred_element_type=jnp.float32)


def pack_kernel(ga_ref, gb_ref, spread_ref, out_ref):
    wide = ga_ref[0:128].T
    narrow = ga_ref[128:192].astype(jnp.float32).T.reshape(REPLICAS, 2, 8, R)
    narrow = jnp.concatenate([narrow[:, 0], narrow[:, 1]], axis=-1)
    gb = gb_ref[...]
    stacked = jnp.concatenate([gb[:, c * 128 : (c + 1) * 128] for c in range(CHUNKS)], axis=0)
    placed = dot(spread_ref[...], stacked).astype(jnp.bfloat16)
    for x in range(NX):
        for y in range(NY):
            at = x * NY + y
            ids = [shard_id(x, y, z) for z in range(NZ)]
            out_ref[at, A1:A2] = jnp.concatenate([wide[16 * d : 16 * d + 16] for d in ids], axis=0)
            out_ref[at, A2:B0] = jnp.concatenate([narrow[d] for d in ids], axis=0).astype(
                jnp.bfloat16
            )
            out_ref[at, B0:PADDED] = placed[at * BROWS : (at + 1) * BROWS]


def partial_kernel(in_ref, pa, pb, ma, mb, sa, sb, out_ref):
    total = in_ref[0].astype(jnp.float32)
    for i in range(1, NP):
        total = total + in_ref[i].astype(jnp.float32)
    pieces = [total[:BLOCK]]
    for ref in (pa, ma, sa):
        pieces.append(jnp.concatenate([ref[0], ref[1]], axis=-1))
    for ref in (pa, ma, sa):
        pieces.append(jnp.concatenate([ref[2, 0:8], ref[2, 8:16]], axis=-1))
    for ref in (pb, mb, sb):
        pieces.append(ref[...])
    pieces.append(jnp.zeros((ROW - OWN3 - 3 * CHUNKS, 128), jnp.float32))
    row = jnp.concatenate(pieces, axis=0)
    for z in range(NZ):
        out_ref[z] = row


def block_mean(in_ref):
    total = in_ref[0, 0:BLOCK]
    for z in range(1, NZ):
        total = total + in_ref[z, 0:BLOCK]
    return total / REPLICAS


def squares_kernel(in_ref, out_ref):
    mean = block_mean(in_ref)
    squares = jnp.sum(mean * mean, axis=0, keepdims=True)
    out_ref[...] = jnp.broadcast_to(squares, out_ref.shape)


def update_kernel(place_ref, squares_ref, in_ref, out_ref, new_a_ref, new_b_ref):
    squares = jnp.sum(squares_ref[...], axis=0, keepdims=True)
    squares = jnp.sum(squares, axis=1, keepdims=True)
    clip = jnp.minimum(1.0, 1.0 / (jnp.sqrt(squares) + 1e-06))
    own = []
    for i in range(3):
        first, second, third = (OWN1 + 16 * i, OWN2 + 8 * i, OWN3 + CHUNKS * i)
        own.append(
            jnp.concatenate(
                [in_ref[z, first : first + 16] for z in range(NZ)]
                + [in_ref[z, second : second + 8] for z in range(NZ)]
                + [in_ref[z, third : third + CHUNKS] for z in range(NZ)],
                axis=0,
            )
        )
    param, moment, second = own
    grad = block_mean(in_ref) * clip
    moment = 0.9 * moment + 0.1 * grad
    second = 0.999 * second + 0.001 * grad * grad
    first_hat = moment / first_fix
    second_hat = second / second_fix
    new = param - 0.1 * first_hat / (jnp.sqrt(second_hat) + 1e-08)
    padded = jnp.concatenate([new, jnp.zeros((PADDED - BLOCK, 128), jnp.float32)], axis=0)
    adapter = padded.astype(jnp.bfloat16)
    for i in range(NP):
        out_ref[i] = adapter
    place = place_ref[0]
    for z in range(NZ):

        @pl.when(place == z)
        def _():
            wide = new[A1 + 16 * z : A1 + 16 * z + 16]
            narrow = new[A2 + 8 * z : A2 + 8 * z + 8]
            new_a_ref[0] = wide[:, :R]
            new_a_ref[1] = wide[:, R:]
            new_a_ref[2, 0:8] = narrow[:, :R]
            new_a_ref[2, 8:16] = narrow[:, R:]
            new_b_ref[...] = new[B0 + CHUNKS * z : B0 + CHUNKS * z + CHUNKS]


def shrink_kernel(group_ref, hidden_ref, in_ref, out_ref):
    del group_ref
    hidden = hidden_ref[...].reshape(TOKENS, D // GROUPS)
    wide, narrow = [], []
    for x in range(NX):
        for z in range(NZ):
            for y in range(NY):
                at = x * NY + y
                wide.append(in_ref[at, A1 + 16 * z : A1 + 16 * z + 16])
    tail = in_ref[:, A2:B0].astype(jnp.float32)
    for x in range(NX):
        for z in range(NZ):
            for y in range(NY):
                piece = tail[x * NY + y, 8 * z : 8 * z + 8]
                narrow += [piece, piece]
    wide = jnp.concatenate(wide, axis=0)
    narrow = jnp.concatenate(narrow, axis=0).astype(jnp.bfloat16)
    lane = lax.broadcasted_iota(jnp.int32, hidden.shape, 1) % 16
    zero = jnp.zeros_like(hidden)
    low = dot(jnp.where(lane < 8, hidden, zero), narrow)
    high = dot(jnp.where(lane < 8, zero, hidden), narrow)
    value = low[:, :R] + high[:, R:]
    value = jnp.concatenate([value[: TOKENS // 2], value[TOKENS // 2 :]], axis=-1)
    partial = jnp.concatenate([dot(hidden, wide), value], axis=0)
    for i in range(GROUPS):
        out_ref[i] = partial


def attend_kernel(
    lengths, parts, adapters, rank, chunk, order, back, base_q, base_kv, keys, values, out_ref
):
    shrink = parts[0]
    for i in range(1, GROUPS):
        shrink = shrink + parts[i]
    value = shrink[TOKENS:]
    value = jnp.concatenate([value[:, :R], value[:, R:]], axis=0)
    stacked = jnp.concatenate([shrink[:TOKENS, :R], shrink[:TOKENS, R:], value], axis=0)
    spread = dot(stacked.astype(jnp.bfloat16), rank[...]).astype(jnp.bfloat16)
    which = chunk[...]
    lhs = []
    for c in range(CHUNKS):
        j = max(0, c - QUERY_PER_KV + 1)
        part = spread[j * TOKENS : (j + 1) * TOKENS]
        lhs.append(jnp.where(which == c, part, jnp.zeros_like(part)))
    rhs = jnp.concatenate([adapters[i, B0:PADDED] for i in range(NP)], axis=0)
    delta = 2.0 * dot(jnp.concatenate(lhs, axis=0), rhs)
    query = []
    for g in range(QUERY_PER_KV):
        base = base_q[:, g * HEAD_SIZE : (g + 1) * HEAD_SIZE].astype(jnp.float32)
        query.append((base + delta[g * TOKENS : (g + 1) * TOKENS]).astype(jnp.bfloat16))
    split = QUERY_PER_KV * TOKENS
    base = base_kv[...].astype(jnp.float32)
    key = (base[:, :HEAD_SIZE] + delta[split : split + TOKENS]).astype(jnp.bfloat16)
    new = (base[:, HEAD_SIZE:] + delta[split + TOKENS :]).astype(jnp.bfloat16)
    query = dot(order[...], jnp.concatenate(query, axis=0)).astype(jnp.bfloat16)
    inv = HEAD_SIZE ** (-0.5)
    fresh = dot_nt(query, key) * inv
    at = lax.broadcasted_iota(jnp.int32, fresh.shape, 0)
    to = lax.broadcasted_iota(jnp.int32, fresh.shape, 1)
    seen = (to % ROWS == at // TOKENS) & (to // ROWS <= at % STEPS)
    fresh = jnp.where(seen, fresh, -jnp.inf)
    slot = lax.broadcasted_iota(jnp.int32, (TOKENS, CACHE), 1)
    outputs = []
    for b in range(ROWS):
        q = query[b * TOKENS : (b + 1) * TOKENS]
        cached = dot_nt(q, keys[b]) * inv
        cached = jnp.where(slot < lengths[b], cached, -jnp.inf)
        late = fresh[b * TOKENS : (b + 1) * TOKENS]
        top = jnp.maximum(
            jnp.max(cached, axis=-1, keepdims=True), jnp.max(late, axis=-1, keepdims=True)
        )
        e_cached = jnp.exp(cached - top)
        e_late = jnp.exp(late - top)
        total = jnp.sum(e_cached, axis=-1, keepdims=True) + jnp.sum(e_late, axis=-1, keepdims=True)
        out = dot(e_cached.astype(jnp.bfloat16), values[b]) + dot(e_late.astype(jnp.bfloat16), new)
        outputs.append((out / total).astype(jnp.bfloat16))
    result = dot(back[...], jnp.concatenate(outputs, axis=0)).astype(jnp.bfloat16)
    for g in range(QUERY_PER_KV):
        out_ref[:, g * HEAD_SIZE : (g + 1) * HEAD_SIZE] = result[g * TOKENS : (g + 1) * TOKENS]


def pack(ga, gb, spread):
    shape = jax.ShapeDtypeStruct((NP, PADDED, 128), jnp.bfloat16)
    return call(pack_kernel, shape, ga, gb, spread)


def partial_row(arrived, *own):
    shape = jax.ShapeDtypeStruct((NZ, ROW, 128), jnp.float32)
    return call(partial_kernel, shape, arrived, *own)


def squares_of(sums):
    shape = jax.ShapeDtypeStruct((NP * GROUPS, 128), jnp.float32)
    return call(squares_kernel, shape, sums)


def update(place, squares, sums):
    shapes = (
        jax.ShapeDtypeStruct((NP, PADDED, 128), jnp.bfloat16),
        jax.ShapeDtypeStruct((3, 16, R), jnp.float32),
        jax.ShapeDtypeStruct((CHUNKS, 128), jnp.float32),
    )
    return call(update_kernel, shapes, place, squares, sums, smem=(0,))


def shrink(group, hidden, adapters):
    width = D // GROUPS
    return pl.pallas_call(
        shrink_kernel,
        out_shape=jax.ShapeDtypeStruct((GROUPS, 48, 128), jnp.float32),
        grid_spec=pltpu.PrefetchScalarGridSpec(
            num_scalar_prefetch=1,
            grid=(1,),
            in_specs=[
                pl.BlockSpec((STEPS, ROWS, width), lambda i, g: (0, 0, g[0])),
                pl.BlockSpec((NP, PADDED, 128), lambda i, g: (0, 0, 0)),
            ],
            out_specs=pl.BlockSpec((GROUPS, 48, 128), lambda i, g: (0, 0, 0)),
        ),
        compiler_params=pltpu.CompilerParams(vmem_limit_bytes=48 * 1024 * 1024),
    )(group, hidden, adapters)


def attend(lengths, parts, adapters, rank, chunk, order, back, base_q, base_kv, keys, values):
    shape = jax.ShapeDtypeStruct((TOKENS, QUERY_PER_KV * HEAD_SIZE), jnp.bfloat16)
    return call(
        attend_kernel, shape, lengths, parts, adapters, rank, chunk, order, back,
        base_q, base_kv, keys, values, smem=(0,),
    )


def natural(a):
    return jnp.transpose(a[0], (1, 0, 2))


def shards(
    grad_a,
    grad_b,
    params_a,
    params_b,
    moment_a,
    moment_b,
    second_a,
    second_b,
    hidden_in,
    base_q,
    base_kv,
    cache_keys,
    cache_values,
    lengths,
):
    spread, rank, chunk, order = tables()
    place = lax.axis_index("zl").reshape(1)
    group = lax.axis_index(TENSOR).reshape(1)
    bf16 = jnp.bfloat16
    ga = jnp.transpose(grad_a[0, 0], (1, 2, 0)).reshape(3 * R, D // GROUPS)
    sent = pack(ga, grad_b[0, :, 0], jnp.asarray(spread, bf16))
    arrived = lax.all_to_all(sent, PLANE, 0, 0, tiled=True)
    own = []
    for a, b in ((params_a, params_b), (moment_a, moment_b), (second_a, second_b)):
        own += [natural(a), b.reshape(CHUNKS, 128)]
    sums = lax.all_to_all(partial_row(arrived, *own), "zl", 0, 0, tiled=True)
    squares = squares_of(sums).reshape(NP * GROUPS, 1, 128)
    squares = lax.all_to_all(squares, PLANE + TENSOR, 0, 0, tiled=True)
    adapters, new_a, new_b = update(place, squares.reshape(NP * GROUPS, 128), sums)
    adapters = lax.all_to_all(adapters, PLANE, 0, 0, tiled=True)
    parts = lax.all_to_all(shrink(group, hidden_in, adapters), TENSOR, 0, 0, tiled=True)
    out = attend(
        lengths,
        parts,
        adapters,
        jnp.asarray(rank, bf16),
        jnp.asarray(chunk),
        jnp.asarray(order, bf16),
        jnp.asarray(order.T, bf16),
        base_q.reshape(TOKENS, -1),
        base_kv.reshape(TOKENS, -1),
        cache_keys.reshape(ROWS, CACHE, HEAD_SIZE),
        cache_values.reshape(ROWS, CACHE, HEAD_SIZE),
    )
    new_a = jnp.transpose(new_a, (1, 0, 2))[None]
    return (out.reshape(STEPS, ROWS, 1, -1), new_a, new_b.reshape(params_b.shape))


def solution(mesh):
    fine = Mesh(mesh.devices.reshape(NX, NZ, NY, 4, 2), DP + TENSOR)
    in_specs = (
        P(DP, TENSOR, None, None, None),
        P(DP, None, TENSOR, None),
        P(TENSOR, DP, None, None),
        P(DP, TENSOR, None),
        P(TENSOR, DP, None, None),
        P(DP, TENSOR, None),
        P(TENSOR, DP, None, None),
        P(DP, TENSOR, None),
        P(None, DP, None),
        P(None, DP, TENSOR, None),
        P(None, DP, TENSOR, None),
        P(DP, TENSOR, None, None),
        P(DP, TENSOR, None, None),
        P(DP),
    )
    out_specs = (
        P(None, DP, TENSOR, None),
        P(TENSOR, DP, None, None),
        P(DP, TENSOR, None),
    )
    return jax.shard_map(shards, mesh=fine, in_specs=in_specs, out_specs=out_specs, check_vma=False)
```

time: 1250 us -> 122 us (0.10)
  the two profiles are of different devices: /device:TPU:8 before, /device:TPU:33 now
where the time goes in v2:
time: 122 us; the launch traced here: 121 us
  waiting for transfers between devices  57.2 us (47%)
  starting transfers between devices  34.9 us (29%)
  blocking collectives  15.4 us (13%)
  Pallas kernels  8.43 us (7%)
  local copies, waits for them, and re-layouts  4.4 us (4%)
    all_to_all x1, starting transfers between devices, shards(): squares = lax.all_to_all(squares, PLANE + TENSOR, 0, 0, tiled=True)  18.7 us
    all_to_all x1, waiting for transfers between devices, shards(): squares = lax.all_to_all(squares, PLANE + TENSOR, 0, 0, tiled=True)  18.1 us
    all_to_all x1, waiting for transfers between devices, shards(): lax.all_to_all(shrink(group, hidden_in, adapters), TENSOR, 0, 0, tiled=True)  17.3 us
    all_to_all x1, blocking collectives, shards(): sums = lax.all_to_all(partial_row(arrived, *own), 'zl', 0, 0, tiled=True)  15.4 us
    all_to_all x1, waiting for transfers between devices, shards(): adapters = lax.all_to_all(adapters, PLANE, 0, 0, tiled=True)  10.9 us
    all_to_all x1, waiting for transfers between devices, shards(): arrived = lax.all_to_all(sent, PLANE, 0, 0, tiled=True)  10.9 us
    pallas_call x5, Pallas kernels, call(): pl.pallas_call(kernel, out_shape=out_shape, in_specs=[scalar if i in smem...  7.41 us
    all_to_all x1, starting transfers between devices, shards(): arrived = lax.all_to_all(sent, PLANE, 0, 0, tiled=True)  6.9 us
  transfers between devices with their start and end apart: 4, of which 4 were waited for; matrix products, arithmetic and copies ran while one was open for 1% of the time, Pallas kernels for 0%

profile of v2, /device:TPU:33, one launch (start us, length us, event | category | flops | bytes accessed | tf_op | source)
XLA Modules:
  0.0 121.2 jit_solution(16117978488336508081)
XLA Ops:
  0.6 0.0 copy-start.2
  0.6 1.2 copy-done.2
  1.8 0.0 copy-start.4
  1.8 1.0 copy-done.4
  2.8 0.0 copy-start.5
  2.8 0.9 copy-done.5
  3.7 1.3 %shard_map.202 = bf16[16,144,128]{2,1,0:T(8,128)(2,1)} custom-call(bf16[192,1024]{1,0:T(8,128)(2,1)S(1)} %bitcast.36, bf16[64,1280]{1,0:T(8,128)(2,1)S(1)} %bitcast.38, bf16[768,640]{1,0:T(8,128)(2,1)S(1)} %copy-done.2), custom_call_target="tpu_custom_call" | custom-call | tf_op jit(solution)/shard_map/pallas_call | solution.py:69
  5.0 0.0 copy-start.16
  5.0 0.0 copy-start.17
  5.0 0.0 copy-start.18
  5.0 0.0 copy-start.12
  5.0 6.9 %all-to-all-start = ((bf16[16,144,128]{2,1,0:T(8,128)(2,1)}), bf16[16,144,128]{2,1,0:T(8,128)(2,1)S(1)}, u32[]{:S(2)}, u32[]{:S(2)}) async-start(bf16[16,144,128]{2,1,0:T(8,128)(2,1)} %shard_map.202), calls=%async_computation | async-start | bytes 1179648 | tf_op jit(solution)/shard_map/all_to_all | solution.py:331
  11.9 0.0 copy-done.16
  11.9 0.0 copy-start.10
  11.9 0.0 copy-start.11
  12.0 0.0 copy-done.17
  12.0 0.0 copy-done.18
  12.1 10.9 %all-to-all-done.in_ref = bf16[16,144,128]{2,1,0:T(8,128)(2,1)S(1)} async-done(((bf16[16,144,128]{2,1,0:T(8,128)(2,1)}), bf16[16,144,128]{2,1,0:T(8,128)(2,1)S(1)}, u32[]{:S(2)}, u32[]{:S(2)}) %all-to-all-start) | async-done | bytes 589856 | tf_op jit(solution)/shard_map/all_to_all | solution.py:331
  22.9 0.0 copy-done.12
  22.9 0.0 copy-done.10
  22.9 0.0 copy-done.11
  22.9 0.1 shard_map.203
  23.0 15.4 %all_to_all.25.in_ref = f32[4,240,128]{2,1,0:T(8,128)S(1)} all-to-all(f32[4,240,128]{2,1,0:T(8,128)S(1)} %shard_map.203), channel_id=1, replica_groups=mesh['x'=4,'zl'=4,'y'=4,'zh'=4,'c'=2] {'zl'}, dimensions={0} | all-to-all | bytes 983040 | tf_op jit(solution)/shard_map/all_to_all | solution.py:335
  38.5 0.7 shard_map.204
  39.1 18.7 %all-to-all-start.2 = ((f32[128,1,128]{2,1,0:T(1,128)}), f32[128,1,128]{2,1,0:T(1,128)S(1)}, u32[]{:S(2)}, u32[]{:S(2)}) async-start(f32[128,1,128]{2,1,0:T(1,128)} %bitcast.13), calls=%async_computation.2 | async-start | bytes 131072 | tf_op jit(solution)/shard_map/all_to_all | solution.py:337
  57.8 18.1 %all-to-all-done.2 = f32[128,1,128]{2,1,0:T(1,128)S(1)} async-done(((f32[128,1,128]{2,1,0:T(1,128)}), f32[128,1,128]{2,1,0:T(1,128)S(1)}, u32[]{:S(2)}, u32[]{:S(2)}) %all-to-all-start.2) | async-done | bytes 65568 | tf_op jit(solution)/shard_map/all_to_all | solution.py:337
  75.9 0.0 copy-start.3
  75.9 1.1 shard_map.205
  77.0 0.0 copy-start.1
  77.0 3.7 %all-to-all-start.3 = ((bf16[16,144,128]{2,1,0:T(8,128)(2,1)}), bf16[16,144,128]{2,1,0:T(8,128)(2,1)S(1)}, u32[]{:S(2)}, u32[]{:S(2)}) async-start(bf16[16,144,128]{2,1,0:T(8,128)(2,1)} %get-tuple-element.6), calls=%async_computation.3 | async-start | bytes 1179648 | tf_op jit(solution)/shard_map/all_to_all | solution.py:339
  80.7 0.0 copy-start
  80.7 10.9 %all-to-all-done.3.in_ref.adapters = bf16[16,144,128]{2,1,0:T(8,128)(2,1)S(1)} async-done(((bf16[16,144,128]{2,1,0:T(8,128)(2,1)}), bf16[16,144,128]{2,1,0:T(8,128)(2,1)S(1)}, u32[]{:S(2)}, u32[]{:S(2)}) %all-to-all-start.3) | async-done | bytes 589856 | tf_op jit(solution)/shard_map/all_to_all | solution.py:339
  91.7 0.0 copy-done.3
  91.7 0.0 copy-start.9
  91.7 1.0 shard_map.206
  92.7 5.6 %all-to-all-start.4 = ((f32[8,48,128]{2,1,0:T(8,128)}), f32[8,48,128]{2,1,0:T(8,128)S(1)}, u32[]{:S(2)}, u32[]{:S(2)}) async-start(f32[8,48,128]{2,1,0:T(8,128)} %shard_map.206), calls=%async_computation.4 | async-start | bytes 393216 | tf_op jit(solution)/shard_map/all_to_all | solution.py:340
  98.3 0.6 reshape.61
  98.9 17.3 %all-to-all-done.4.parts = f32[8,48,128]{2,1,0:T(8,128)S(1)} async-done(((f32[8,48,128]{2,1,0:T(8,128)}), f32[8,48,128]{2,1,0:T(8,128)S(1)}, u32[]{:S(2)}, u32[]{:S(2)}) %all-to-all-start.4) | async-done | bytes 196640 | tf_op jit(solution)/shard_map/all_to_all | solution.py:340
  116.2 0.0 copy-done.1
  116.2 0.0 copy-done
  116.2 0.0 copy-done.9
  116.2 0.0 copy-done.6
  116.2 0.0 copy-done.7
  116.3 0.0 copy-done.8
  116.3 0.0 copy-done.13
  116.3 0.6 copy-done.14
  116.9 0.0 copy-done.15
  116.9 4.3 %shard_map.207 = bf16[32,1024]{1,0:T(8,128)(2,1)} custom-call(s32[8]{0:T(128)S(1)} %copy-done.15, f32[8,48,128]{2,1,0:T(8,128)S(1)} %all-to-all-done.4.parts, bf16[16,144,128]{2,1,0:T(8,128)(2,1)S(1)} %all-to-all-done.3.in_ref.adapters, bf16[64,768]{1,0:T(8,128)(2,1)S(1)} %copy-done.8, s32[1,768]{1,0:T(1,128)S(1)} %copy-done.14, ...), custom_call_target="tpu_custom_call" | custom-call | tf_op jit(solution)/shard_map/pallas_call | solution.py:69
  (9 shorter events, 0.1 us)
Async XLA Ops:
  0.6 1.2 copy-start.2
  1.8 1.0 copy-start.4
  2.8 0.9 copy-start.5
  5.0 6.9 %copy-start.16 = (f32[1,1,1280]{2,1,0:T(1,128)S(1)}, f32[1,1,1280]{2,1,0:T(1,128)}, u32[]{:S(2)}) copy-start(f32[1,1,1280]{2,1,0:T(1,128)} %param.22) | copy-start | bytes 15364
  5.0 7.0 %copy-start.17 = (f32[1,1,1280]{2,1,0:T(1,128)S(1)}, f32[1,1,1280]{2,1,0:T(1,128)}, u32[]{:S(2)}) copy-start(f32[1,1,1280]{2,1,0:T(1,128)} %param.24) | copy-start | bytes 15364
  5.0 7.0 %copy-start.18 = (f32[1,1,1280]{2,1,0:T(1,128)S(1)}, f32[1,1,1280]{2,1,0:T(1,128)}, u32[]{:S(2)}) copy-start(f32[1,1,1280]{2,1,0:T(1,128)} %param.26) | copy-start | bytes 15364
  5.0 17.9 %copy-start.12 = (f32[1,16,3,64]{3,1,2,0:T(8,128)S(1)}, f32[1,16,3,64]{3,1,2,0:T(8,128)}, u32[]{:S(2)}) copy-start(f32[1,16,3,64]{3,1,2,0:T(8,128)} %param.25) | copy-start | bytes 36868
  5.0 17.9 %all-to-all-start = ((bf16[16,144,128]{2,1,0:T(8,128)(2,1)}), bf16[16,144,128]{2,1,0:T(8,128)(2,1)S(1)}, u32[]{:S(2)}, u32[]{:S(2)}) async-start(bf16[16,144,128]{2,1,0:T(8,128)(2,1)} %shard_map.202), calls=%async_computation | async-start | bytes 1179648 | tf_op jit(solution)/shard_map/all_to_all | solution.py:331
  11.9 11.0 %copy-start.10 = (f32[1,16,3,64]{3,1,2,0:T(8,128)S(1)}, f32[1,16,3,64]{3,1,2,0:T(8,128)}, u32[]{:S(2)}) copy-start(f32[1,16,3,64]{3,1,2,0:T(8,128)} %param.21) | copy-start | bytes 36868
  11.9 11.0 %copy-start.11 = (f32[1,16,3,64]{3,1,2,0:T(8,128)S(1)}, f32[1,16,3,64]{3,1,2,0:T(8,128)}, u32[]{:S(2)}) copy-start(f32[1,16,3,64]{3,1,2,0:T(8,128)} %param.23) | copy-start | bytes 36868
  39.1 36.8 %all-to-all-start.2 = ((f32[128,1,128]{2,1,0:T(1,128)}), f32[128,1,128]{2,1,0:T(1,128)S(1)}, u32[]{:S(2)}, u32[]{:S(2)}) async-start(f32[128,1,128]{2,1,0:T(1,128)} %bitcast.13), calls=%async_computation.2 | async-start | bytes 131072 | tf_op jit(solution)/shard_map/all_to_all | solution.py:337
  75.9 15.7 %copy-start.3 = (bf16[4,8,8192]{2,1,0:T(8,128)(2,1)S(1)}, bf16[4,8,8192]{2,1,0:T(8,128)(2,1)}, u32[]{:S(2)}) copy-start(bf16[4,8,8192]{2,1,0:T(8,128)(2,1)} %hidden_ref.1) | copy-start | bytes 1572868
  77.0 39.2 %copy-start.1 = (bf16[8,1,512,128]{3,2,1,0:T(8,128)(2,1)S(1)}, bf16[8,1,512,128]{3,2,1,0:T(8,128)(2,1)}, u32[]{:S(2)}) copy-start(bf16[8,1,512,128]{3,2,1,0:T(8,128)(2,1)} %param.31) | copy-start | bytes 3145732
  77.0 14.6 %all-to-all-start.3 = ((bf16[16,144,128]{2,1,0:T(8,128)(2,1)}), bf16[16,144,128]{2,1,0:T(8,128)(2,1)S(1)}, u32[]{:S(2)}, u32[]{:S(2)}) async-start(bf16[16,144,128]{2,1,0:T(8,128)(2,1)} %get-tuple-element.6), calls=%async_computation.3 | async-start | bytes 1179648 | tf_op jit(solution)/shard_map/all_to_all | solution.py:339
  80.7 35.5 %copy-start = (bf16[8,1,512,128]{3,2,1,0:T(8,128)(2,1)S(1)}, bf16[8,1,512,128]{3,2,1,0:T(8,128)(2,1)}, u32[]{:S(2)}) copy-start(bf16[8,1,512,128]{3,2,1,0:T(8,128)(2,1)} %param.30) | copy-start | bytes 3145732
  91.7 24.6 %copy-start.9 = (bf16[4,8,1,1024]{3,1,2,0:T(8,128)(2,1)S(1)}, bf16[4,8,1,1024]{3,1,2,0:T(8,128)(2,1)}, u32[]{:S(2)}) copy-start(bf16[4,8,1,1024]{3,1,2,0:T(8,128)(2,1)} %param.28) | copy-start | bytes 196612
  92.7 23.6 %copy-start.6 = (bf16[256,256]{1,0:T(8,128)(2,1)S(1)}, bf16[256,256]{1,0:T(8,128)(2,1)}, u32[]{:S(2)}) copy-start(bf16[256,256]{1,0:T(8,128)(2,1)} %constant.28.clone.back) | copy-start | bytes 393220
  92.7 23.6 %copy-start.7 = (bf16[256,256]{1,0:T(8,128)(2,1)S(1)}, bf16[256,256]{1,0:T(8,128)(2,1)}, u32[]{:S(2)}) copy-start(bf16[256,256]{1,0:T(8,128)(2,1)} %constant.27.clone.order) | copy-start | bytes 393220
  92.7 23.6 %copy-start.8 = (bf16[64,768]{1,0:T(8,128)(2,1)S(1)}, bf16[64,768]{1,0:T(8,128)(2,1)}, u32[]{:S(2)}) copy-start(bf16[64,768]{1,0:T(8,128)(2,1)} %constant.25.clone.rank) | copy-start | bytes 294916
  92.7 23.5 %all-to-all-start.4 = ((f32[8,48,128]{2,1,0:T(8,128)}), f32[8,48,128]{2,1,0:T(8,128)S(1)}, u32[]{:S(2)}, u32[]{:S(2)}) async-start(f32[8,48,128]{2,1,0:T(8,128)} %shard_map.206), calls=%async_computation.4 | async-start | bytes 393216 | tf_op jit(solution)/shard_map/all_to_all | solution.py:340
  98.3 18.0 %copy-start.13 = (bf16[4,8,1,256]{3,1,2,0:T(8,128)(2,1)S(1)}, bf16[4,8,1,256]{3,1,2,0:T(8,128)(2,1)}, u32[]{:S(2)}) copy-start(bf16[4,8,1,256]{3,1,2,0:T(8,128)(2,1)} %param.29) | copy-start | bytes 49156
  116.2 0.7 copy-start.14
  116.2 0.7 copy-start.15

commit v3 on v2

v3 whole, which is shorter than its diff:
```python
import jax
import jax.numpy as jnp
from jax import lax
from jax.experimental import pallas as pl
from jax.experimental.pallas import tpu as pltpu
from jax.sharding import Mesh
from jax.sharding import PartitionSpec as P

D = 8192
R = 64
QUERY_PER_KV = 8
HEAD_SIZE = 128
STEPS = 4
ROWS = 8
CACHE = 512
TOKENS = STEPS * ROWS
REPLICAS = 64
GROUPS = 8

first_fix = 0.9999734386011124
second_fix = 0.09520785288629038

DP = ("x", "zl", "y")
TENSOR = ("zh", "c")
PLANE = ("x", "y")
NX, NZ, NY = 4, 4, 4
NP = NX * NY

A1, A2, B0 = 0, 64, 96
BLOCK = 136
PADDED = 144
BROWS = PADDED - B0
CHUNKS = 10
OWN1, OWN2, OWN3 = 136, 184, 208
ROW = 240


def shard_id(x, y, z):
    return (x * NZ + z) * NY + y


def call(kernel, out_shape, *args, smem=(), scratch=()):
    vmem = pl.BlockSpec(memory_space=pltpu.VMEM)
    scalar = pl.BlockSpec(memory_space=pltpu.SMEM)
    many = isinstance(out_shape, (tuple, list))
    return pl.pallas_call(
        kernel,
        out_shape=out_shape,
        in_specs=[scalar if i in smem else vmem for i in range(len(args))],
        out_specs=[vmem] * len(out_shape) if many else vmem,
        scratch_shapes=scratch,
        compiler_params=pltpu.CompilerParams(vmem_limit_bytes=48 * 1024 * 1024),
    )(*args)


def dot(a, b):
    return jnp.dot(a, b, preferred_element_type=jnp.float32)


def dot_nt(a, b):
    return lax.dot_general(a, b, (((1,), (1,)), ((), ())), preferred_element_type=jnp.float32)


def one_hot(shape, column_of):
    row = lax.broadcasted_iota(jnp.int32, shape, 0)
    column = lax.broadcasted_iota(jnp.int32, shape, 1)
    return (column_of(row) == column).astype(jnp.float32).astype(jnp.bfloat16)


def pack_kernel(ga_ref, gb_ref, out_ref, rows_ref):
    turn = one_hot((REPLICAS, R), lambda i: ((i // (NY * NZ)) * NZ + i % NZ) * NY + i // NZ % NY)
    turned = dot(turn, gb_ref[...])
    for c in range(CHUNKS):
        rows_ref[pl.ds(c, REPLICAS, stride=CHUNKS), :] = turned[:, c * 128 : (c + 1) * 128]
    wide = ga_ref[0:128].T
    narrow = ga_ref[128:192].astype(jnp.float32).T.reshape(REPLICAS, 2, 8, R)
    narrow = jnp.concatenate([narrow[:, 0], narrow[:, 1]], axis=-1)
    count = NZ * CHUNKS
    none = jnp.zeros((PADDED - BLOCK, 128), jnp.float32)
    for x in range(NX):
        for y in range(NY):
            at = x * NY + y
            ids = [shard_id(x, y, z) for z in range(NZ)]
            out_ref[at, A1:A2] = jnp.concatenate([wide[16 * d : 16 * d + 16] for d in ids], axis=0)
            tail = [narrow[d] for d in ids] + [rows_ref[at * count : (at + 1) * count], none]
            out_ref[at, A2:PADDED] = jnp.concatenate(tail, axis=0).astype(jnp.bfloat16)


def partial_kernel(in_ref, pa, pb, ma, mb, sa, sb, out_ref):
    total = in_ref[0].astype(jnp.float32)
    for i in range(1, NP):
        total = total + in_ref[i].astype(jnp.float32)
    pieces = [total[:BLOCK]]
    for ref in (pa, ma, sa):
        pieces.append(jnp.concatenate([ref[0], ref[1]], axis=-1))
    for ref in (pa, ma, sa):
        pieces.append(jnp.concatenate([ref[2, 0:8], ref[2, 8:16]], axis=-1))
    for ref in (pb, mb, sb):
        pieces += [ref[0, :, c * 128 : (c + 1) * 128] for c in range(CHUNKS)]
    pieces.append(jnp.zeros((ROW - OWN3 - 3 * CHUNKS, 128), jnp.float32))
    row = jnp.concatenate(pieces, axis=0)
    for z in range(NZ):
        out_ref[z] = row


def block_mean(in_ref):
    total = in_ref[0, 0:BLOCK]
    for z in range(1, NZ):
        total = total + in_ref[z, 0:BLOCK]
    return total / REPLICAS


def squares_kernel(in_ref, out_ref):
    mean = block_mean(in_ref)
    squares = jnp.sum(mean * mean, axis=0, keepdims=True)
    out_ref[...] = jnp.broadcast_to(squares, out_ref.shape)


def update_kernel(squares_ref, in_ref, out_ref, new_a_ref, new_b_ref):
    squares = jnp.sum(squares_ref[...], axis=0, keepdims=True)
    squares = jnp.sum(squares, axis=1, keepdims=True)
    clip = jnp.minimum(1.0, 1.0 / (jnp.sqrt(squares) + 1e-06))
    own = []
    for i in range(3):
        first, second, third = (OWN1 + 16 * i, OWN2 + 8 * i, OWN3 + CHUNKS * i)
        own.append(
            jnp.concatenate(
                [in_ref[z, first : first + 16] for z in range(NZ)]
                + [in_ref[z, second : second + 8] for z in range(NZ)]
                + [in_ref[z, third : third + CHUNKS] for z in range(NZ)],
                axis=0,
            )
        )
    param, moment, second = own
    grad = block_mean(in_ref) * clip
    moment = 0.9 * moment + 0.1 * grad
    second = 0.999 * second + 0.001 * grad * grad
    first_hat = moment / first_fix
    second_hat = second / second_fix
    new = param - 0.1 * first_hat / (jnp.sqrt(second_hat) + 1e-08)
    padded = jnp.concatenate([new, jnp.zeros((PADDED - BLOCK, 128), jnp.float32)], axis=0)
    adapter = padded.astype(jnp.bfloat16)
    for i in range(NP):
        out_ref[i] = adapter
    place = lax.axis_index("zl")
    for z in range(NZ):

        @pl.when(place == z)
        def _():
            wide = new[A1 + 16 * z : A1 + 16 * z + 16]
            narrow = new[A2 + 8 * z : A2 + 8 * z + 8]
            new_a_ref[0] = wide[:, :R]
            new_a_ref[1] = wide[:, R:]
            new_a_ref[2, 0:8] = narrow[:, :R]
            new_a_ref[2, 8:16] = narrow[:, R:]
            for c in range(CHUNKS):
                row = B0 + CHUNKS * z + c
                new_b_ref[0, :, c * 128 : (c + 1) * 128] = new[row : row + 1]


def shrink_kernel(hidden_ref, in_ref, out_ref):
    width = D // GROUPS
    group = lax.axis_index("zh") * 2 + lax.axis_index("c")
    start = pl.multiple_of(group * width, width)
    hidden = hidden_ref[:, :, pl.ds(start, width)].reshape(TOKENS, width)
    wide, narrow = [], []
    for x in range(NX):
        for z in range(NZ):
            for y in range(NY):
                at = x * NY + y
                wide.append(in_ref[at, A1 + 16 * z : A1 + 16 * z + 16])
    tail = in_ref[:, A2:B0].astype(jnp.float32)
    for x in range(NX):
        for z in range(NZ):
            for y in range(NY):
                piece = tail[x * NY + y, 8 * z : 8 * z + 8]
                narrow += [piece, piece]
    wide = jnp.concatenate(wide, axis=0)
    narrow = jnp.concatenate(narrow, axis=0).astype(jnp.bfloat16)
    lane = lax.broadcasted_iota(jnp.int32, hidden.shape, 1) % 16
    zero = jnp.zeros_like(hidden)
    low = dot(jnp.where(lane < 8, hidden, zero), narrow)
    high = dot(jnp.where(lane < 8, zero, hidden), narrow)
    value = low[:, :R] + high[:, R:]
    value = jnp.concatenate([value[: TOKENS // 2], value[TOKENS // 2 :]], axis=-1)
    partial = jnp.concatenate([dot(hidden, wide), value], axis=0)
    for i in range(GROUPS):
        out_ref[i] = partial


def attend_kernel(
    lengths, parts, adapters, base_q, base_kv, keys, values, out_ref
):
    shrink = parts[0]
    for i in range(1, GROUPS):
        shrink = shrink + parts[i]
    value = shrink[TOKENS:]
    value = jnp.concatenate([value[:, :R], value[:, R:]], axis=0)
    stacked = jnp.concatenate([shrink[:TOKENS, :R], shrink[:TOKENS, R:], value], axis=0)
    shape = (R, NP * BROWS)
    row = lax.broadcasted_iota(jnp.int32, (1, NP * BROWS), 1)
    at, inside = row // BROWS, row % BROWS
    real = inside < NZ * CHUNKS
    owner = jnp.where(real, ((at // NY) * NZ + inside // CHUNKS) * NY + at % NY, -1)
    rank = (lax.broadcasted_iota(jnp.int32, shape, 0) == owner).astype(jnp.float32)
    spread = dot(stacked.astype(jnp.bfloat16), rank.astype(jnp.bfloat16)).astype(jnp.bfloat16)
    which = jnp.where(real, inside % CHUNKS, -1)
    lhs = []
    for c in range(CHUNKS):
        j = max(0, c - QUERY_PER_KV + 1)
        part = spread[j * TOKENS : (j + 1) * TOKENS]
        lhs.append(jnp.where(which == c, part, jnp.zeros_like(part)))
    rhs = jnp.concatenate([adapters[i, B0:PADDED] for i in range(NP)], axis=0)
    delta = 2.0 * dot(jnp.concatenate(lhs, axis=0), rhs)
    query = []
    for g in range(QUERY_PER_KV):
        base = base_q[:, g * HEAD_SIZE : (g + 1) * HEAD_SIZE].astype(jnp.float32)
        query.append((base + delta[g * TOKENS : (g + 1) * TOKENS]).astype(jnp.bfloat16))
    split = QUERY_PER_KV * TOKENS
    base = base_kv[...].astype(jnp.float32)
    key = (base[:, :HEAD_SIZE] + delta[split : split + TOKENS]).astype(jnp.bfloat16)
    new = (base[:, HEAD_SIZE:] + delta[split + TOKENS :]).astype(jnp.bfloat16)
    size = (QUERY_PER_KV * TOKENS,) * 2
    order = one_hot(size, lambda i: (i % TOKENS) * ROWS + i // TOKENS)
    back = one_hot(size, lambda i: (i % ROWS) * TOKENS + i // ROWS)
    query = dot(order, jnp.concatenate(query, axis=0)).astype(jnp.bfloat16)
    inv = HEAD_SIZE ** (-0.5)
    fresh = dot_nt(query, key) * inv
    at = lax.broadcasted_iota(jnp.int32, fresh.shape, 0)
    to = lax.broadcasted_iota(jnp.int32, fresh.shape, 1)
    seen = (to % ROWS == at // TOKENS) & (to // ROWS <= at % STEPS)
    fresh = jnp.where(seen, fresh, -jnp.inf)
    slot = lax.broadcasted_iota(jnp.int32, (TOKENS, CACHE), 1)
    spans = [slice(b * TOKENS, (b + 1) * TOKENS) for b in range(ROWS)]
    cached = []
    for b in range(ROWS):
        part = dot_nt(query[spans[b]], keys[b]) * inv
        cached.append(jnp.where(slot < lengths[b], part, -jnp.inf))
    cached = jnp.concatenate(cached, axis=0)
    top = jnp.maximum(
        jnp.max(cached, axis=-1, keepdims=True), jnp.max(fresh, axis=-1, keepdims=True)
    )
    e_cached = jnp.exp(cached - top)
    e_fresh = jnp.exp(fresh - top)
    total = jnp.sum(e_cached, axis=-1, keepdims=True) + jnp.sum(e_fresh, axis=-1, keepdims=True)
    weights = e_cached.astype(jnp.bfloat16)
    out = jnp.concatenate([dot(weights[spans[b]], values[b]) for b in range(ROWS)], axis=0)
    out = out + dot(e_fresh.astype(jnp.bfloat16), new)
    result = dot(back, (out / total).astype(jnp.bfloat16)).astype(jnp.bfloat16)
    for g in range(QUERY_PER_KV):
        out_ref[:, g * HEAD_SIZE : (g + 1) * HEAD_SIZE] = result[g * TOKENS : (g + 1) * TOKENS]


def pack(ga, gb):
    shape = jax.ShapeDtypeStruct((NP, PADDED, 128), jnp.bfloat16)
    scratch = [pltpu.VMEM((R * CHUNKS, 128), jnp.float32)]
    return call(pack_kernel, shape, ga, gb, scratch=scratch)


def partial_row(arrived, *own):
    shape = jax.ShapeDtypeStruct((NZ, ROW, 128), jnp.float32)
    return call(partial_kernel, shape, arrived, *own)


def squares_of(sums):
    shape = jax.ShapeDtypeStruct((NP * GROUPS, 128), jnp.float32)
    return call(squares_kernel, shape, sums)


def update(squares, sums):
    shapes = (
        jax.ShapeDtypeStruct((NP, PADDED, 128), jnp.bfloat16),
        jax.ShapeDtypeStruct((3, 16, R), jnp.float32),
        jax.ShapeDtypeStruct((1, 1, CHUNKS * 128), jnp.float32),
    )
    return call(update_kernel, shapes, squares, sums)


def shrink(hidden, adapters):
    shape = jax.ShapeDtypeStruct((GROUPS, 48, 128), jnp.float32)
    return call(shrink_kernel, shape, hidden, adapters)


def attend(lengths, parts, adapters, base_q, base_kv, keys, values):
    shape = jax.ShapeDtypeStruct((TOKENS, QUERY_PER_KV * HEAD_SIZE), jnp.bfloat16)
    return call(
        attend_kernel, shape, lengths, parts, adapters, base_q, base_kv, keys, values, smem=(0,)
    )


def natural(a):
    return jnp.transpose(a[0], (1, 0, 2))


def shards(
    grad_a,
    grad_b,
    params_a,
    params_b,
    moment_a,
    moment_b,
    second_a,
    second_b,
    hidden_in,
    base_q,
    base_kv,
    cache_keys,
    cache_values,
    lengths,
):
    ga = jnp.transpose(grad_a[0, 0], (1, 2, 0)).reshape(3 * R, D // GROUPS)
    sent = pack(ga, grad_b[0, :, 0])
    arrived = lax.all_to_all(sent, PLANE, 0, 0, tiled=True)
    own = []
    for a, b in ((params_a, params_b), (moment_a, moment_b), (second_a, second_b)):
        own += [natural(a), b]
    sums = lax.all_to_all(partial_row(arrived, *own), "zl", 0, 0, tiled=True)
    squares = squares_of(sums).reshape(NP * GROUPS, 1, 128)
    squares = lax.all_to_all(squares, PLANE + TENSOR, 0, 0, tiled=True)
    adapters, new_a, new_b = update(squares.reshape(NP * GROUPS, 128), sums)
    adapters = lax.all_to_all(adapters, PLANE, 0, 0, tiled=True)
    parts = lax.all_to_all(shrink(hidden_in, adapters), TENSOR, 0, 0, tiled=True)
    out = attend(
        lengths,
        parts,
        adapters,
        base_q.reshape(TOKENS, -1),
        base_kv.reshape(TOKENS, -1),
        cache_keys.reshape(ROWS, CACHE, HEAD_SIZE),
        cache_values.reshape(ROWS, CACHE, HEAD_SIZE),
    )
    new_a = jnp.transpose(new_a, (1, 0, 2))[None]
    return (out.reshape(STEPS, ROWS, 1, -1), new_a, new_b)


def solution(mesh):
    fine = Mesh(mesh.devices.reshape(NX, NZ, NY, 4, 2), DP + TENSOR)
    in_specs = (
        P(DP, TENSOR, None, None, None),
        P(DP, None, TENSOR, None),
        P(TENSOR, DP, None, None),
        P(DP, TENSOR, None),
        P(TENSOR, DP, None, None),
        P(DP, TENSOR, None),
        P(TENSOR, DP, None, None),
        P(DP, TENSOR, None),
        P(None, DP, None),
        P(None, DP, TENSOR, None),
        P(None, DP, TENSOR, None),
        P(DP, TENSOR, None, None),
        P(DP, TENSOR, None, None),
        P(DP),
    )
    out_specs = (
        P(None, DP, TENSOR, None),
        P(TENSOR, DP, None, None),
        P(DP, TENSOR, None),
    )
    return jax.shard_map(shards, mesh=fine, in_specs=in_specs, out_specs=out_specs, check_vma=False)
```

time: 122 us -> 115 us (0.943)
  blocking collectives: 15.4 us -> 106 us
  waiting for transfers between devices: 57.2 us -> 0 us
  starting transfers between devices: 34.9 us -> 0 us
  Pallas kernels: 8.43 us -> 4.45 us
    all_to_all x0 -> x4, blocking collectives: none -> 90.8 us  [the longest x1 36.7 us: shards(): squares = lax.all_to_all(squares, PLANE + TENSOR, 0, 0, tiled=True)]
    all_to_all x4 -> x0, waiting for transfers between devices: 57.2 us -> none  [the longest x1 18.1 us: shards(): squares = lax.all_to_all(squares, PLANE + TENSOR, 0, 0, tiled=True)]
    all_to_all x4 -> x0, starting transfers between devices: 34.9 us -> none  [the longest x1 18.7 us: shards(): squares = lax.all_to_all(squares, PLANE + TENSOR, 0, 0, tiled=True)]
    pallas_call x5 -> x6, Pallas kernels: 7.41 us -> 4.45 us  [call(): pl.pallas_call(kernel, out_shape=out_shape, in_specs=[scalar if i in smem...]
    unnamed x38 -> x28, local copies, waits for them, and re-layouts: 3.79 us -> 3.25 us
  transfers between devices with their start and end apart: 4 -> 0, of which waited for: 4 -> 0; matrix products, arithmetic and copies ran while one was open for 1% -> 0% of each run, Pallas kernels for 0% -> 0%
where the time goes in v3:
time: 115 us
  blocking collectives  106 us (92%)
  Pallas kernels  4.45 us (4%)
  local copies, waits for them, and re-layouts  3.25 us (3%)
    all_to_all x1, blocking collectives, shards(): squares = lax.all_to_all(squares, PLANE + TENSOR, 0, 0, tiled=True)  36.7 us
    all_to_all x1, blocking collectives, shards(): lax.all_to_all(shrink(hidden_in, adapters), TENSOR, 0, 0, tiled=True)  22.6 us
    all_to_all x1, blocking collectives, shards(): arrived = lax.all_to_all(sent, PLANE, 0, 0, tiled=True)  17.7 us
    all_to_all x1, blocking collectives, shards(): sums = lax.all_to_all(partial_row(arrived, *own), 'zl', 0, 0, tiled=True)  15.4 us
    all_to_all x1, blocking collectives, shards(): adapters = lax.all_to_all(adapters, PLANE, 0, 0, tiled=True)  13.9 us
    pallas_call x6, Pallas kernels, call(): pl.pallas_call(kernel, out_shape=out_shape, in_specs=[scalar if i in smem...  4.45 us
    unnamed x28, local copies, waits for them, and re-layouts  3.25 us

profile of v3, /device:TPU:33, one launch (start us, length us, event | category | flops | bytes accessed | tf_op | source)
XLA Modules:
  0.0 114.7 jit_solution(8624516205460576653)
XLA Ops:
  0.6 0.0 copy-start.3
  0.6 1.0 copy-done.3
  1.6 0.0 copy-start.4
  1.6 0.9 copy-done.4
  2.5 0.3 shard_map.157
  2.9 0.0 copy-start.6
  2.9 0.0 copy-start.7
  2.9 0.0 copy-start.8
  2.9 0.0 copy-start.11
  2.9 0.0 copy-start.12
  2.9 17.7 %all_to_all.25.in_ref = bf16[16,144,128]{2,1,0:T(8,128)(2,1)S(1)} all-to-all(bf16[16,144,128]{2,1,0:T(8,128)(2,1)S(1)} %shard_map.157), channel_id=1, replica_groups=mesh['x'=4,'zl'=4,'y'=4,'zh'=4,'c'=2] {'x','y'}, dimensions={0} | all-to-all | bytes 1179648 | tf_op jit(solution)/shard_map/all_to_all | solution.py:313
  20.6 0.0 copy-start.10
  20.6 0.0 copy-done.6
  20.6 0.0 copy-done.7
  20.6 0.0 copy-done.8
  20.6 0.0 copy-done.11
  20.6 0.0 copy-done.12
  20.6 0.7 copy-done.10
  21.3 0.1 shard_map.158
  21.4 15.4 %all_to_all.26.in_ref = f32[4,240,128]{2,1,0:T(8,128)S(1)} all-to-all(f32[4,240,128]{2,1,0:T(8,128)S(1)} %shard_map.158), channel_id=1, replica_groups=mesh['x'=4,'zl'=4,'y'=4,'zh'=4,'c'=2] {'zl'}, dimensions={0} | all-to-all | bytes 983040 | tf_op jit(solution)/shard_map/all_to_all | solution.py:317
  36.8 36.7 %all_to_all.27 = f32[128,1,128]{2,1,0:T(1,128)S(1)} all-to-all(f32[128,1,128]{2,1,0:T(1,128)S(1)} %bitcast.33), channel_id=1, replica_groups=mesh['x'=4,'zl'=4,'y'=4,'zh'=4,'c'=2] {'x','y','zh','c'}, dimensions={0} | all-to-all | bytes 131072 | tf_op jit(solution)/shard_map/all_to_all | solution.py:319
  73.5 0.0 copy-start.2
  73.5 0.9 shard_map.160
  74.4 0.0 copy-start.1
  74.4 13.9 %all_to_all.28.in_ref.adapters = bf16[16,144,128]{2,1,0:T(8,128)(2,1)S(1)} all-to-all(bf16[16,144,128]{2,1,0:T(8,128)(2,1)S(1)} %get-tuple-element.6), channel_id=1, replica_groups=mesh['x'=4,'zl'=4,'y'=4,'zh'=4,'c'=2] {'x','y'}, dimensions={0} | all-to-all | bytes 1179648 | tf_op jit(solution)/shard_map/all_to_all | solution.py:321
  88.3 0.0 copy-done.2
  88.3 0.0 copy-start
  88.3 0.3 shard_map.161
  88.6 0.0 copy-start.5
  88.6 0.0 copy-start.9
  88.6 22.6 %all_to_all.29.parts = f32[8,48,128]{2,1,0:T(8,128)S(1)} all-to-all(f32[8,48,128]{2,1,0:T(8,128)S(1)} %shard_map.161), channel_id=1, replica_groups=mesh['x'=4,'zl'=4,'y'=4,'zh'=4,'c'=2] {'zh','c'}, dimensions={0} | all-to-all | bytes 393216 | tf_op jit(solution)/shard_map/all_to_all | solution.py:322
  111.2 0.0 copy-start.13
  111.2 0.0 copy-done.1
  111.2 0.0 copy-done
  111.2 0.0 copy-done.5
  111.2 0.0 copy-done.9
  111.3 0.6 copy-done.13
  111.9 2.8 %shard_map.162 = bf16[32,1024]{1,0:T(8,128)(2,1)} custom-call(s32[8]{0:T(128)S(1)} %copy-done.13, f32[8,48,128]{2,1,0:T(8,128)S(1)} %all_to_all.29.parts, bf16[16,144,128]{2,1,0:T(8,128)(2,1)S(1)} %all_to_all.28.in_ref.adapters, bf16[32,1024]{1,0:T(8,128)(2,1)S(1)} %bitcast.35, bf16[32,256]{1,0:T(8,128)(2,1)S(1)} %bitcast.39, ...), custom_call_target="tpu_custom_call" | custom-call | tf_op jit(solution)/shard_map/pallas_call | solution.py:46
  (1 shorter events, 0.0 us)
Async XLA Ops:
  0.6 1.0 copy-start.3
  1.6 0.9 copy-start.4
  2.9 17.7 %copy-start.6 = (f32[1,16,3,64]{3,1,2,0:T(8,128)S(1)}, f32[1,16,3,64]{3,1,2,0:T(8,128)}, u32[]{:S(2)}) copy-start(f32[1,16,3,64]{3,1,2,0:T(8,128)} %param.16) | copy-start | bytes 36868
  2.9 17.7 %copy-start.7 = (f32[1,16,3,64]{3,1,2,0:T(8,128)S(1)}, f32[1,16,3,64]{3,1,2,0:T(8,128)}, u32[]{:S(2)}) copy-start(f32[1,16,3,64]{3,1,2,0:T(8,128)} %param.18) | copy-start | bytes 36868
  2.9 17.7 %copy-start.8 = (f32[1,16,3,64]{3,1,2,0:T(8,128)S(1)}, f32[1,16,3,64]{3,1,2,0:T(8,128)}, u32[]{:S(2)}) copy-start(f32[1,16,3,64]{3,1,2,0:T(8,128)} %param.20) | copy-start | bytes 36868
  2.9 17.7 %copy-start.11 = (f32[1,1,1280]{2,1,0:T(1,128)S(1)}, f32[1,1,1280]{2,1,0:T(1,128)}, u32[]{:S(2)}) copy-start(f32[1,1,1280]{2,1,0:T(1,128)} %mb.1) | copy-start | bytes 15364
  2.9 17.7 %copy-start.12 = (f32[1,1,1280]{2,1,0:T(1,128)S(1)}, f32[1,1,1280]{2,1,0:T(1,128)}, u32[]{:S(2)}) copy-start(f32[1,1,1280]{2,1,0:T(1,128)} %sb.1) | copy-start | bytes 15364
  20.6 0.7 copy-start.10
  73.5 14.8 %copy-start.2 = (bf16[4,8,8192]{2,1,0:T(8,128)(2,1)S(1)}, bf16[4,8,8192]{2,1,0:T(8,128)(2,1)}, u32[]{:S(2)}) copy-start(bf16[4,8,8192]{2,1,0:T(8,128)(2,1)} %hidden_ref.1) | copy-start | bytes 1572868
  74.4 36.9 %copy-start.1 = (bf16[8,1,512,128]{3,2,1,0:T(8,128)(2,1)S(1)}, bf16[8,1,512,128]{3,2,1,0:T(8,128)(2,1)}, u32[]{:S(2)}) copy-start(bf16[8,1,512,128]{3,2,1,0:T(8,128)(2,1)} %param.26) | copy-start | bytes 3145732
  88.3 23.0 %copy-start = (bf16[8,1,512,128]{3,2,1,0:T(8,128)(2,1)S(1)}, bf16[8,1,512,128]{3,2,1,0:T(8,128)(2,1)}, u32[]{:S(2)}) copy-start(bf16[8,1,512,128]{3,2,1,0:T(8,128)(2,1)} %param.25) | copy-start | bytes 3145732
  88.6 22.6 %copy-start.5 = (bf16[4,8,1,1024]{3,1,2,0:T(8,128)(2,1)S(1)}, bf16[4,8,1,1024]{3,1,2,0:T(8,128)(2,1)}, u32[]{:S(2)}) copy-start(bf16[4,8,1,1024]{3,1,2,0:T(8,128)(2,1)} %param.23) | copy-start | bytes 196612
  88.6 22.6 %copy-start.9 = (bf16[4,8,1,256]{3,1,2,0:T(8,128)(2,1)S(1)}, bf16[4,8,1,256]{3,1,2,0:T(8,128)(2,1)}, u32[]{:S(2)}) copy-start(bf16[4,8,1,256]{3,1,2,0:T(8,128)(2,1)} %param.24) | copy-start | bytes 49156
  111.2 0.7 copy-start.13
